TPU v7x, 32 devices: a whole 2x2x4 slice. The times are simulated.
32 devices in a mesh: grp: 2 (over x), gx: 16 (over z, y, core).
Axes of the slice: x: 2, y: 2, z: 4, core: 2. Of those that a mesh axis runs over, the one named last changes fastest.
Arguments:
- layer_input: bfloat16 [512, 9216], P(('grp', 'gx')), parts along dimension 0, may hold values from -6 to 6
- norm_gain: float32 [9216], replicated, may hold values from 0.1 to 1.9
- w_query: bfloat16 [9216, 6144], P(None, 'gx'), may hold values from -2 to 2
- w_keyval: bfloat16 [9216, 512], P(None, 'gx'), may hold values from -0.0625 to 0.0625
- w_out: bfloat16 [6144, 9216], P('gx'), may hold values from -0.078125 to 0.078125
- w_gate: bfloat16 [9216, 9216], P(None, 'gx'), may hold values from -0.0625 to 0.0625
- w_up: bfloat16 [9216, 9216], P(None, 'gx'), may hold values from -0.0625 to 0.0625
- w_down: bfloat16 [9216, 9216], P('gx'), may hold values from -0.0625 to 0.0625
- cache_keys: bfloat16 [512, 256, 256], P(('grp', 'gx')), parts along dimension 0, may hold values from -6 to 6
- cache_values: bfloat16 [512, 256, 256], P(('grp', 'gx')), parts along dimension 0, may hold values from -6 to 6
- lengths: int32 [512], P(('grp', 'gx')), parts along dimension 0, may hold values from 2 to 256, as said below
Outputs:
- layer_output: bfloat16 [512, 9216], P(('grp', 'gx')), parts along dimension 0
There are 2 independent parts, one for each index of `grp`. A program takes and returns all parts, laid end to end along the dimension named above; an argument that names none is the same for every part. Nothing has to cross between parts.
Inputs may be any that keep to these rules, and one draw needn't show every extreme that they name: `lengths`: each row's count of cached tokens; some row of every replica holds all 256.
All inputs are finite; a program needn't handle non-finite values.
Results may differ from a plain program's by a relative error of at most 0.0057.
Values may be sent and summed in bfloat16 or wider, within the bound.
A program may use at most 192 MiB of HBM per device.

v0:
```python
import jax
import jax.numpy as jnp
from jax import lax
from jax.sharding import PartitionSpec as P

H = 24
HD = 256


def block_scores(queries, key_block, lengths):
    scores = (
        jnp.einsum("rhd,rld->rhl", queries, key_block, preferred_element_type=jnp.float32) / 16.0
    )
    places = jnp.arange(key_block.shape[1], dtype=jnp.int32)
    live_mask = places[None, :] < lengths[:, None]
    return jnp.where(live_mask[:, None, :], scores, -1e30)


def attend_all(queries, new_key, new_value, cache_keys, cache_values, lengths):
    scores = block_scores(queries, cache_keys, lengths)
    own_score = (
        jnp.einsum("rhd,rd->rh", queries, new_key, preferred_element_type=jnp.float32) / 16.0
    )
    highest = jnp.maximum(jnp.max(scores, axis=2), own_score)
    weights = jnp.exp(scores - highest[:, :, None])
    own_weight = jnp.exp(own_score - highest)
    denominator = jnp.sum(weights, axis=2) + own_weight
    probs = (weights / denominator[:, :, None]).astype(jnp.bfloat16)
    own_prob = (own_weight / denominator).astype(jnp.bfloat16).astype(jnp.float32)
    attended = jnp.einsum("rhl,rld->rhd", probs, cache_values, preferred_element_type=jnp.float32)
    return attended + own_prob[:, :, None] * new_value.astype(jnp.float32)[:, None, :]


def shards(
    layer_input,
    norm_gain,
    w_query,
    w_keyval,
    w_out,
    w_gate,
    w_up,
    w_down,
    cache_keys,
    cache_values,
    lengths,
):
    row_count = layer_input.shape[0]
    widened = layer_input.astype(jnp.float32)
    row_mean = jnp.mean(widened, axis=1, keepdims=True)
    centred = widened - row_mean
    row_var = jnp.mean(centred * centred, axis=1, keepdims=True)
    normed = (centred * lax.rsqrt(row_var + 1e-06) * norm_gain).astype(jnp.bfloat16)
    gathered = lax.all_gather(normed, "gx", axis=0, tiled=True)
    query_cols = jnp.dot(gathered, w_query, preferred_element_type=jnp.float32).astype(jnp.bfloat16)
    keyval_cols = jnp.dot(gathered, w_keyval, preferred_element_type=jnp.float32).astype(
        jnp.bfloat16
    )
    query_rows, keyval_rows = (
        lax.all_to_all(query_cols, "gx", split_axis=0, concat_axis=1, tiled=True),
        lax.all_to_all(keyval_cols, "gx", split_axis=0, concat_axis=1, tiled=True),
    )
    queries = query_rows.reshape(row_count, H, HD)
    new_key = keyval_rows[:, :HD]
    new_value = keyval_rows[:, HD:]
    attended = attend_all(queries, new_key, new_value, cache_keys, cache_values, lengths)
    attended = attended.reshape(row_count, H * HD).astype(jnp.bfloat16)
    attended_cols = lax.all_to_all(attended, "gx", split_axis=1, concat_axis=0, tiled=True)
    gate_sum = jnp.dot(gathered, w_gate, preferred_element_type=jnp.float32)
    up_sum = jnp.dot(gathered, w_up, preferred_element_type=jnp.float32)
    hidden = (jax.nn.silu(gate_sum) * up_sum).astype(jnp.bfloat16)
    picked = attended_cols
    attention_sum = lax.psum_scatter(
        jnp.dot(picked, w_out, preferred_element_type=jnp.float32),
        "gx",
        scatter_dimension=0,
        tiled=True,
    )
    picked = hidden
    forward_sum = lax.psum_scatter(
        jnp.dot(picked, w_down, preferred_element_type=jnp.float32),
        "gx",
        scatter_dimension=0,
        tiled=True,
    )
    branch_sum = attention_sum + forward_sum
    return (widened + branch_sum).astype(jnp.bfloat16)


def solution(mesh):
    return jax.shard_map(
        shards,
        mesh=mesh,
        in_specs=(
            P(("grp", "gx"), None),
            P(),
            P(None, "gx"),
            P(None, "gx"),
            P("gx", None),
            P(None, "gx"),
            P(None, "gx"),
            P("gx", None),
            P(("grp", "gx"), None, None),
            P(("grp", "gx"), None, None),
            P(("grp", "gx")),
        ),
        out_specs=P(("grp", "gx"), None),
        check_vma=False,
    )
```

profile of v0, /device:TPU:0, one launch (start us, length us, event | category | flops | bytes accessed | tf_op | source)
XLA Modules:
  0.0 262.5 jit_solution(6787039709159300769)
XLA Ops:
  6.5 1.3 convert_reduce_fusion
  7.8 1.2 fusion.5
  9.1 1.8 fusion.7
  10.9 0.0 all-gather.2.cloned.1.call-update
  10.9 0.7 iota_compare_fusion
  11.7 55.5 %all-gather.2.cloned.1.call-done = bf16[256,9216]{1,0:T(8,128)(2,1)} async-done(((bf16[16,9216]{1,0:T(8,128)(2,1)}), bf16[256,9216]{1,0:T(8,128)(2,1)}) %all-gather.2.cloned.1.call-update) | async-done | bytes 4718608 | tf_op jit(solution)/shard_map/all_gather | solution.py:53
  67.2 4.0 %convolution_convert_fusion.1 = bf16[256,32]{0,1:T(8,128)(2,1)S(1)} fusion(bf16[256,9216]{1,0:T(8,128)(2,1)} %all-gather.2.cloned.1.call-done, bf16[9216,32]{0,1:T(8,128)(2,1)} %param.14), kind=kOutput, calls=%fused_computation.8 | convolution fusion | flops 151003136 | bytes 5324800 | tf_op jit(solution)/shard_map/dot_general | solution.py:55
  71.2 0.1 copy.14
  71.3 0.7 reshape.53
  72.0 3.4 %all-to-all-start.1 = ((bf16[16,2,256]{2,1,0:T(2,128)(2,1)}), bf16[16,2,256]{2,1,0:T(2,128)(2,1)S(1)}, u32[]{:S(2)}, u32[]{:S(2)}) async-start(bf16[16,2,256]{2,1,0:T(2,128)(2,1)} %reshape.53), calls=%async_computation.1 | async-start | bytes 32768 | tf_op jit(solution)/shard_map/all_to_all | solution.py:60
  75.5 7.7 %convolution_convert_fusion = bf16[256,384]{1,0:T(8,128)(2,1)} fusion(bf16[256,9216]{1,0:T(8,128)(2,1)} %all-gather.2.cloned.1.call-done, bf16[9216,384]{1,0:T(8,128)(2,1)} %param.13), kind=kOutput, calls=%fused_computation.7 | convolution fusion | flops 1812037632 | bytes 11993088 | tf_op jit(solution)/shard_map/dot_general | solution.py:54
  83.2 0.0 all-to-all-done.1
  83.2 6.0 %all-to-all-start = ((bf16[16,16,384]{2,1,0:T(8,128)(2,1)}), bf16[16,16,384]{2,1,0:T(8,128)(2,1)S(1)}, u32[]{:S(2)}, u32[]{:S(2)}) async-start(bf16[16,16,384]{2,1,0:T(8,128)(2,1)} %bitcast), calls=%async_computation | async-start | bytes 393216 | tf_op jit(solution)/shard_map/all_to_all | solution.py:59
  89.2 7.1 %fusion.20 = f32[256,576]{0,1:T(8,128)S(1)} fusion(bf16[256,9216]{1,0:T(8,128)(2,1)} %all-gather.2.cloned.1.call-done, bf16[9216,576]{0,1:T(8,128)(2,1)} %param.16), kind=kOutput, calls=%fused_computation.39 | convolution fusion | flops 2717908992 | bytes 15925248 | tf_op jit(solution)/shard_map/dot_general | solution.py:68
  96.3 0.1 reshape.54
  96.5 0.1 all_to_all.44
  96.6 1.6 all-to-all-done
  98.2 0.1 reshape.50
  98.4 0.2 fusion.14
  98.5 0.7 fusion.19
  99.3 0.2 fusion.10
  99.6 2.0 fusion.2
  101.6 0.1 convert_element_type.46
  101.7 0.7 copy.16
  102.5 4.4 %all-to-all-start.2 = ((bf16[16,16,384]{2,0,1:T(8,128)(2,1)}), bf16[16,16,384]{2,0,1:T(8,128)(2,1)S(1)}, u32[]{:S(2)}, u32[]{:S(2)}) async-start(bf16[16,16,384]{2,0,1:T(8,128)(2,1)} %copy.16), calls=%async_computation.2 | async-start | bytes 393216 | tf_op jit(solution)/shard_map/all_to_all | solution.py:67
  106.9 0.2 reduce-scatter.2.cloned.1.call-start
  107.1 24.2 %fusion.9 = f32[256,9216]{1,0:T(8,128)} fusion(bf16[576,9216]{1,0:T(8,128)(2,1)} %param.18, bf16[256,9216]{1,0:T(8,128)(2,1)} %all-gather.2.cloned.1.call-done, bf16[9216,576]{0,1:T(8,128)(2,1)} %param.17, f32[256,576]{0,1:T(8,128)S(1)} %fusion.20), kind=kOutput, calls=%fused_computation.18 | convolution fusion | flops 5436702720 | bytes 35979264 | tf_op jit(solution)/shard_map/dot_general | solution.py:80
  131.4 0.0 all-to-all-done.2
  131.4 9.6 %convolution_add_fusion = f32[256,9216]{1,0:T(8,128)} fusion(f32[256,9216]{1,0:T(8,128)} %fusion.9, bf16[256,384]{1,0:T(8,128)(2,1)S(1)} %bitcast.26, bf16[384,9216]{1,0:T(8,128)(2,1)} %param.15), kind=kOutput, calls=%fused_computation | convolution fusion | flops 1814298624 | bytes 26148864 | tf_op jit(solution)/shard_map/dot_general | solution.py:73
  141.0 0.0 reduce-scatter.2.cloned.1.call-update
  141.0 112.8 %reduce-scatter.2.cloned.1.call-done = f32[16,9216]{1,0:T(8,128)} async-done(((f32[256,9216]{1,0:T(8,128)}), f32[16,9216]{1,0:T(8,128)}) %reduce-scatter.2.cloned.1.call-update) | async-done | bytes 589840 | tf_op jit(solution)/shard_map/reduce_scatter | solution.py:72
  253.8 1.8 fusion.8
  (14 shorter events, 0.1 us)
Async XLA Ops:
  6.5 92.0 %copy-start = (bf16[16,256,256]{2,1,0:T(8,128)(2,1)S(1)}, bf16[16,256,256]{2,1,0:T(8,128)(2,1)}, u32[]{:S(2)}) copy-start(bf16[16,256,256]{2,1,0:T(8,128)(2,1)} %param.19) | copy-start | bytes 6291460
  6.5 60.6 %all-gather.2.cloned.1.call-start = ((), (), s32[]{:S(2)}) async-start(), calls=%async_computation.4 | async-start | bytes 5013504 | tf_op jit(solution)/shard_map/all_gather | solution.py:53
  72.0 11.2 %all-to-all-start.1 = ((bf16[16,2,256]{2,1,0:T(2,128)(2,1)}), bf16[16,2,256]{2,1,0:T(2,128)(2,1)S(1)}, u32[]{:S(2)}, u32[]{:S(2)}) async-start(bf16[16,2,256]{2,1,0:T(2,128)(2,1)} %reshape.53), calls=%async_computation.1 | async-start | bytes 32768 | tf_op jit(solution)/shard_map/all_to_all | solution.py:60
  83.2 15.0 %all-to-all-start = ((bf16[16,16,384]{2,1,0:T(8,128)(2,1)}), bf16[16,16,384]{2,1,0:T(8,128)(2,1)S(1)}, u32[]{:S(2)}, u32[]{:S(2)}) async-start(bf16[16,16,384]{2,1,0:T(8,128)(2,1)} %bitcast), calls=%async_computation | async-start | bytes 393216 | tf_op jit(solution)/shard_map/all_to_all | solution.py:59
  102.5 28.9 %all-to-all-start.2 = ((bf16[16,16,384]{2,0,1:T(8,128)(2,1)}), bf16[16,16,384]{2,0,1:T(8,128)(2,1)S(1)}, u32[]{:S(2)}, u32[]{:S(2)}) async-start(bf16[16,16,384]{2,0,1:T(8,128)(2,1)} %copy.16), calls=%async_computation.2 | async-start | bytes 393216 | tf_op jit(solution)/shard_map/all_to_all | solution.py:67
  106.9 146.9 %reduce-scatter.2.cloned.1.call-start = ((), (), s32[]{:S(2)}) async-start(), calls=%async_computation.5 | async-start | bytes 10027008 | tf_op jit(solution)/shard_map/reduce_scatter | solution.py:72
  131.4 124.3 %copy-start.1 = (bf16[16,256,256]{2,1,0:T(8,128)(2,1)S(1)}, bf16[16,256,256]{2,1,0:T(8,128)(2,1)}, u32[]{:S(2)}) copy-start(bf16[16,256,256]{2,1,0:T(8,128)(2,1)} %param.19) | copy-start | bytes 6291460
  141.0 112.8 %copy-start.2 = (bf16[16,9216]{1,0:T(8,128)(2,1)S(1)}, bf16[16,9216]{1,0:T(8,128)(2,1)}, u32[]{:S(2)}) copy-start(bf16[16,9216]{1,0:T(8,128)(2,1)} %param.11) | copy-start | bytes 884740
Sparse Core Ops, SparseCore 0:
  11.1 56.0 all-gather.1
  141.1 112.6 reduce-scatter.1
where the time goes:
time: 263 us; the launch traced here: 262 us
  waiting for transfers between devices  170 us (65%)
  matrix products  55.6 us (21%)
  starting transfers between devices  14.1 us (5%)
  between operations  13.5 us (5%)
  other arithmetic  7.2 us (3%)
    reduce_scatter x1, waiting for transfers between devices, shards(): lax.psum_scatter(jnp.dot(picked, w_out, preferred_element_type=jnp.float3...  113 us
    all_gather x1, waiting for transfers between devices, shards(): gathered = lax.all_gather(normed, 'gx', axis=0, tiled=True)  55.5 us
    dot_general x1, matrix products, shards(): jnp.dot(picked, w_down, preferred_element_type=jnp.float32)  24.2 us
    dot_general x1, matrix products, shards(): jnp.dot(picked, w_out, preferred_element_type=jnp.float32)  9.6 us
    dot_general x1, matrix products, shards(): jnp.dot(gathered, w_query, preferred_element_type=jnp.float32)  7.75 us
    dot_general x1, matrix products, shards(): gate_sum = jnp.dot(gathered, w_gate, preferred_element_type=jnp.float32)  7.12 us
    all_to_all x1, starting transfers between devices, shards(): lax.all_to_all(query_cols, 'gx', split_axis=0, concat_axis=1, tiled=True)  5.97 us
  transfers between devices with their start and end apart: 5, of which 3 were waited for; matrix products, arithmetic and copies ran while one was open for 15% of the time, Pallas kernels for 0%

commit v1 on v0

v1 whole, which is shorter than its diff:
```python
import functools

import jax
import jax.numpy as jnp
from jax import lax
from jax.experimental import pallas as pl
from jax.experimental.pallas import tpu as pltpu
from jax.sharding import PartitionSpec as P

H = 24
HD = 256
MIB = 1024 * 1024


def places(Z):
    me = lax.axis_index("gx")
    z = lax.div(me, 4)
    y = lax.rem(lax.div(me, 2), 2)
    c = lax.rem(me, 2)
    return z, y, c


def index_of(z, y, c):
    return (z * 2 + y) * 2 + c


def partners(Z, z, y, c):
    out = [index_of(lax.rem(z + d, Z), y, c) for d in range(1, Z)]
    return out + [index_of(z, 1 - y, c), index_of(z, y, 1 - c)]


def greet(Z, z, y, c):
    barrier = pltpu.get_barrier_semaphore()
    for p in partners(Z, z, y, c):
        pl.semaphore_signal(
            barrier, inc=1, device_id={"gx": p}, device_id_type=pl.DeviceIdType.MESH
        )
    return barrier


def remote(src, dst, send, recv, p):
    return pltpu.make_async_remote_copy(
        src_ref=src,
        dst_ref=dst,
        send_sem=send,
        recv_sem=recv,
        device_id={"gx": p},
        device_id_type=pl.DeviceIdType.MESH,
    )


def project_kernel(
    Z, R, C, Kc,
    x_ref, gain_ref, wq, wkv, wg, wu,
    q_out, kv_out, hid_out,
    gbuf, wqb, wkvb, wgb, wub, accq, acckv, accg, accu,
    zsend, zrecv, ysend, yrecv, csend, crecv, wsem,
):
    z, y, c = places(Z)
    barrier = greet(Z, z, y, c)
    weights = ((wq, wqb), (wkv, wkvb), (wg, wgb), (wu, wub))
    AHEAD = 4
    LY, LC = 2, 1

    def wcopy(k, i):
        src, dst = weights[i]
        return pltpu.make_async_copy(
            src.at[pl.ds(pl.multiple_of(k * Kc, Kc), Kc), :], dst.at[k], wsem.at[k, i]
        )

    def wstart(k):
        for i in range(4):
            wcopy(k, i).start()

    for k in range(min(AHEAD, C)):
        wstart(k)

    D = C * Kc
    total = jnp.zeros((R, 1), jnp.float32)
    for k in range(C):
        total += jnp.sum(x_ref[:, k * Kc : (k + 1) * Kc].astype(jnp.float32), axis=1, keepdims=True)
    mean = total / D
    square = jnp.zeros((R, 1), jnp.float32)
    for k in range(C):
        centred = x_ref[:, k * Kc : (k + 1) * Kc].astype(jnp.float32) - mean
        square += jnp.sum(centred * centred, axis=1, keepdims=True)
    scale = lax.rsqrt(square / D + 1e-06)

    line = pl.multiple_of((c * 2 + y) * Z * R, R)
    other_line = pl.multiple_of((c * 2 + 1 - y) * Z * R, R)
    half = pl.multiple_of(c * 2 * Z * R, R)
    other_half = pl.multiple_of((1 - c) * 2 * Z * R, R)
    own = pl.multiple_of(((c * 2 + y) * Z + z) * R, R)
    for k in range(C):
        cols = slice(k * Kc, (k + 1) * Kc)
        centred = x_ref[:, cols].astype(jnp.float32) - mean
        gbuf[k, pl.ds(own, R), :] = (centred * scale * gain_ref[:, cols]).astype(jnp.bfloat16)

    def zcopy(k, d):
        ref = gbuf.at[k, pl.ds(own, R), :]
        return remote(
            ref, ref, zsend.at[k, d - 1], zrecv.at[k, d - 1], index_of(lax.rem(z + d, Z), y, c)
        )

    def zarrival(k, d):
        src = pl.multiple_of(((c * 2 + y) * Z + lax.rem(z + Z - d, Z)) * R, R)
        ref = gbuf.at[k, pl.ds(src, R), :]
        return remote(
            ref, ref, zsend.at[k, d - 1], zrecv.at[k, d - 1], index_of(lax.rem(z + d, Z), y, c)
        )

    def ycopy(k, base):
        ref = gbuf.at[k, pl.ds(base, Z * R), :]
        return remote(ref, ref, ysend.at[k], yrecv.at[k], index_of(z, 1 - y, c))

    def ccopy(k, base):
        ref = gbuf.at[k, pl.ds(base, 2 * Z * R), :]
        return remote(ref, ref, csend.at[k], crecv.at[k], index_of(z, y, 1 - c))

    accq[...] = jnp.zeros_like(accq)
    acckv[...] = jnp.zeros_like(acckv)
    accg[...] = jnp.zeros_like(accg)
    accu[...] = jnp.zeros_like(accu)

    pl.semaphore_wait(barrier, Z + 1)
    for k in range(min(2, C)):
        for d in range(1, Z):
            zcopy(k, d).start()

    def step(s, carry):
        @pl.when(s + AHEAD < C)
        def _():
            wstart(s + AHEAD)

        @pl.when(s + 2 < C)
        def _():
            for d in range(1, Z):
                zcopy(s + 2, d).start()

        @pl.when(s < C)
        def _():
            for d in range(1, Z):
                zarrival(s, d).wait_recv()
            ycopy(s, line).start()

        @pl.when(jnp.logical_and(s >= LY, s < C + LY))
        def _():
            k = s - LY
            ycopy(k, other_line).wait_recv()
            ccopy(k, half).start()

        @pl.when(s >= LY + LC)
        def _():
            k = s - LY - LC
            ccopy(k, other_half).wait_recv()
            for i in range(4):
                wcopy(k, i).wait()
            rows = gbuf[k]
            for acc, w in ((accq, wqb), (acckv, wkvb), (accg, wgb), (accu, wub)):
                acc[...] += jnp.dot(rows, w[k], preferred_element_type=jnp.float32)

        return carry

    lax.fori_loop(0, C + LY + LC, step, 0)

    q_out[...] = accq[...].astype(jnp.bfloat16)
    kv_out[...] = acckv[...].astype(jnp.bfloat16)
    gate = accg[...]
    hid_out[...] = (gate * jax.nn.sigmoid(gate) * accu[...]).astype(jnp.bfloat16)

    def drain(k, carry):
        for d in range(1, Z):
            zcopy(k, d).wait_send()
        ycopy(k, line).wait_send()
        ccopy(k, half).wait_send()
        return carry

    lax.fori_loop(0, C, drain, 0)


def project(n, x, gain, wq, wkv, wg, wu):
    R, D = x.shape
    Z = n // 4
    Kc = 1024
    C = D // Kc
    N = n * R
    nq, nkv, ng = wq.shape[1], wkv.shape[1], wg.shape[1]
    vmem = pl.BlockSpec(memory_space=pltpu.VMEM)
    hbm = pl.BlockSpec(memory_space=pl.ANY)
    bf, f32 = jnp.bfloat16, jnp.float32
    return pl.pallas_call(
        functools.partial(project_kernel, Z, R, C, Kc),
        out_shape=[
            jax.ShapeDtypeStruct((N, nq), bf),
            jax.ShapeDtypeStruct((N, nkv), bf),
            jax.ShapeDtypeStruct((N, ng), bf),
        ],
        in_specs=[vmem, vmem, hbm, hbm, hbm, hbm],
        out_specs=[vmem, vmem, vmem],
        scratch_shapes=[
            pltpu.VMEM((C, N, Kc), bf),
            pltpu.VMEM((C, Kc, nq), bf),
            pltpu.VMEM((C, Kc, nkv), bf),
            pltpu.VMEM((C, Kc, ng), bf),
            pltpu.VMEM((C, Kc, ng), bf),
            pltpu.VMEM((N, nq), f32),
            pltpu.VMEM((N, nkv), f32),
            pltpu.VMEM((N, ng), f32),
            pltpu.VMEM((N, ng), f32),
            pltpu.SemaphoreType.DMA((C, Z - 1)),
            pltpu.SemaphoreType.DMA((C, Z - 1)),
            pltpu.SemaphoreType.DMA((C,)),
            pltpu.SemaphoreType.DMA((C,)),
            pltpu.SemaphoreType.DMA((C,)),
            pltpu.SemaphoreType.DMA((C,)),
            pltpu.SemaphoreType.DMA((C, 4)),
        ],
        compiler_params=pltpu.CompilerParams(
            collective_id=0, has_side_effects=True, vmem_limit_bytes=56 * MIB
        ),
        name="project",
    )(x, gain.reshape(1, D), wq, wkv, wg, wu)


def combine_kernel(
    Z, R, C, Kc,
    x_ref, lhs_ref, wo, wd,
    out_ref,
    wbuf, part, lineb, ownb, csb, crb, ysb, yrb, zsb, zrb,
    zsend, zrecv, ysend, yrecv, csend, crecv, wsem,
):
    z, y, c = places(Z)
    barrier = greet(Z, z, y, c)
    no, nd = wo.shape[0], wd.shape[0]
    AHEAD = 4
    LC, LY, LZ = 1, 2, 2

    def wcopies(k):
        cols = pl.ds(pl.multiple_of(k * Kc, Kc), Kc)
        return (
            pltpu.make_async_copy(wo.at[:, cols], wbuf.at[k, pl.ds(0, no), :], wsem.at[k, 0]),
            pltpu.make_async_copy(wd.at[:, cols], wbuf.at[k, pl.ds(no, nd), :], wsem.at[k, 1]),
        )

    def wstart(k):
        for copy in wcopies(k):
            copy.start()

    for k in range(min(AHEAD, C)):
        wstart(k)

    half = pl.multiple_of(c * 2 * Z * R, R)
    other_half = pl.multiple_of((1 - c) * 2 * Z * R, R)
    line = pl.multiple_of(y * Z * R, R)
    other_line = pl.multiple_of((1 - y) * Z * R, R)
    own = pl.multiple_of(z * R, R)

    def ccopy(k):
        return remote(csb.at[k], crb.at[k], csend.at[k], crecv.at[k], index_of(z, y, 1 - c))

    def ycopy(k):
        return remote(ysb.at[k], yrb.at[k], ysend.at[k], yrecv.at[k], index_of(z, 1 - y, c))

    def zcopy(k, d):
        to = lax.rem(z + d, Z)
        return remote(
            zsb.at[k, pl.ds(pl.multiple_of(to * R, R), R), :],
            zrb.at[k, d - 1],
            zsend.at[k, d - 1],
            zrecv.at[k, d - 1],
            index_of(to, y, c),
        )

    pl.semaphore_wait(barrier, Z + 1)

    def step(s, carry):
        @pl.when(s + AHEAD < C)
        def _():
            wstart(s + AHEAD)

        @pl.when(s < C)
        def _():
            for copy in wcopies(s):
                copy.wait()
            slot = lax.rem(s, 4)
            part[slot] = jnp.dot(lhs_ref[...], wbuf[s], preferred_element_type=jnp.float32)
            csb[s] = part[slot, pl.ds(other_half, 2 * Z * R), :].astype(jnp.bfloat16)
            ccopy(s).start()

        @pl.when(jnp.logical_and(s >= LC, s < C + LC))
        def _():
            k = s - LC
            slot = lax.rem(k, 4)
            ccopy(k).wait_recv()
            ysb[k] = (
                part[slot, pl.ds(half + other_line, Z * R), :]
                + crb[k, pl.ds(other_line, Z * R), :].astype(jnp.float32)
            ).astype(jnp.bfloat16)
            ycopy(k).start()
            lineb[slot] = part[slot, pl.ds(half + line, Z * R), :] + crb[
                k, pl.ds(line, Z * R), :
            ].astype(jnp.float32)

        @pl.when(jnp.logical_and(s >= LC + LY, s < C + LC + LY))
        def _():
            k = s - LC - LY
            slot = lax.rem(k, 4)
            ycopy(k).wait_recv()
            lineb[slot] = lineb[slot] + yrb[k].astype(jnp.float32)
            zsb[k] = lineb[slot].astype(jnp.bfloat16)
            for d in range(1, Z):
                zcopy(k, d).start()
            ownb[slot] = lineb[slot, pl.ds(own, R), :]

        @pl.when(s >= LC + LY + LZ)
        def _():
            k = s - LC - LY - LZ
            slot = lax.rem(k, 4)
            cols = pl.ds(pl.multiple_of(k * Kc, Kc), Kc)
            total = ownb[slot]
            for d in range(1, Z):
                zcopy(k, d).wait_recv()
                total = total + zrb[k, d - 1].astype(jnp.float32)
            out_ref[:, cols] = (x_ref[:, cols].astype(jnp.float32) + total).astype(jnp.bfloat16)

        return carry

    lax.fori_loop(0, C + LC + LY + LZ, step, 0)

    def drain(k, carry):
        for d in range(1, Z):
            zcopy(k, d).wait_send()
        ycopy(k).wait_send()
        ccopy(k).wait_send()
        return carry

    lax.fori_loop(0, C, drain, 0)


def combine(n, x, lhs, wo, wd):
    R, D = x.shape
    Z = n // 4
    Kc = 1024
    C = D // Kc
    N = n * R
    vmem = pl.BlockSpec(memory_space=pltpu.VMEM)
    hbm = pl.BlockSpec(memory_space=pl.ANY)
    bf, f32 = jnp.bfloat16, jnp.float32
    return pl.pallas_call(
        functools.partial(combine_kernel, Z, R, C, Kc),
        out_shape=jax.ShapeDtypeStruct((R, D), bf),
        in_specs=[vmem, vmem, hbm, hbm],
        out_specs=vmem,
        scratch_shapes=[
            pltpu.VMEM((C, lhs.shape[1], Kc), bf),
            pltpu.VMEM((4, N, Kc), f32),
            pltpu.VMEM((4, Z * R, Kc), f32),
            pltpu.VMEM((4, R, Kc), f32),
            pltpu.VMEM((C, N // 2, Kc), bf),
            pltpu.VMEM((C, N // 2, Kc), bf),
            pltpu.VMEM((C, Z * R, Kc), bf),
            pltpu.VMEM((C, Z * R, Kc), bf),
            pltpu.VMEM((C, Z * R, Kc), bf),
            pltpu.VMEM((C, Z - 1, R, Kc), bf),
            pltpu.SemaphoreType.DMA((C, Z - 1)),
            pltpu.SemaphoreType.DMA((C, Z - 1)),
            pltpu.SemaphoreType.DMA((C,)),
            pltpu.SemaphoreType.DMA((C,)),
            pltpu.SemaphoreType.DMA((C,)),
            pltpu.SemaphoreType.DMA((C,)),
            pltpu.SemaphoreType.DMA((C, 2)),
        ],
        compiler_params=pltpu.CompilerParams(
            collective_id=1, has_side_effects=True, vmem_limit_bytes=56 * MIB
        ),
        name="combine",
    )(x, lhs, wo, wd)


def block_scores(queries, key_block, lengths):
    scores = (
        jnp.einsum("rhd,rld->rhl", queries, key_block, preferred_element_type=jnp.float32) / 16.0
    )
    places = jnp.arange(key_block.shape[1], dtype=jnp.int32)
    live_mask = places[None, :] < lengths[:, None]
    return jnp.where(live_mask[:, None, :], scores, -1e30)


def attend_all(queries, new_key, new_value, cache_keys, cache_values, lengths):
    scores = block_scores(queries, cache_keys, lengths)
    own_score = (
        jnp.einsum("rhd,rd->rh", queries, new_key, preferred_element_type=jnp.float32) / 16.0
    )
    highest = jnp.maximum(jnp.max(scores, axis=2), own_score)
    weights = jnp.exp(scores - highest[:, :, None])
    own_weight = jnp.exp(own_score - highest)
    denominator = jnp.sum(weights, axis=2) + own_weight
    probs = (weights / denominator[:, :, None]).astype(jnp.bfloat16)
    own_prob = (own_weight / denominator).astype(jnp.bfloat16).astype(jnp.float32)
    attended = jnp.einsum("rhl,rld->rhd", probs, cache_values, preferred_element_type=jnp.float32)
    return attended + own_prob[:, :, None] * new_value.astype(jnp.float32)[:, None, :]


def shards(
    n,
    layer_input,
    norm_gain,
    w_query,
    w_keyval,
    w_out,
    w_gate,
    w_up,
    w_down,
    cache_keys,
    cache_values,
    lengths,
):
    R = layer_input.shape[0]
    Z = n // 4
    query_cols, keyval_cols, hidden = project(
        n, layer_input, norm_gain, w_query, w_keyval, w_gate, w_up
    )

    def to_index_order(a):
        a = a.reshape(2, 2, Z, R, a.shape[1]).transpose(2, 1, 0, 3, 4)
        return a.reshape(n, R, a.shape[4])

    query_rows, keyval_rows = (
        lax.all_to_all(to_index_order(query_cols), "gx", split_axis=0, concat_axis=0, tiled=True),
        lax.all_to_all(to_index_order(keyval_cols), "gx", split_axis=0, concat_axis=0, tiled=True),
    )
    queries = query_rows.transpose(1, 0, 2).reshape(R, H, HD)
    keyval_rows = keyval_rows.transpose(1, 0, 2).reshape(R, 2 * HD)
    new_key = keyval_rows[:, :HD]
    new_value = keyval_rows[:, HD:]
    attended = attend_all(queries, new_key, new_value, cache_keys, cache_values, lengths)
    attended = attended.reshape(R, H * HD).astype(jnp.bfloat16)
    att = lax.all_to_all(
        attended.reshape(R, n, -1).transpose(1, 0, 2), "gx", split_axis=0, concat_axis=0, tiled=True
    )
    att = att.reshape(Z, 2, 2, R, -1).transpose(2, 1, 0, 3, 4).reshape(n * R, -1)
    lhs = jnp.concatenate([att, hidden], axis=1)
    return combine(n, layer_input, lhs, w_out, w_down)


def solution(mesh):
    n = mesh.shape["gx"]
    return jax.shard_map(
        functools.partial(shards, n),
        mesh=mesh,
        in_specs=(
            P(("grp", "gx"), None),
            P(),
            P(None, "gx"),
            P(None, "gx"),
            P("gx", None),
            P(None, "gx"),
            P(None, "gx"),
            P("gx", None),
            P(("grp", "gx"), None, None),
            P(("grp", "gx"), None, None),
            P(("grp", "gx")),
        ),
        out_specs=P(("grp", "gx"), None),
        check_vma=False,
    )
```

time: 263 us -> 158 us (0.60)
  waiting for transfers between devices: 170 us -> 13.5 us
  Pallas kernels: 0 us -> 81.2 us
  matrix products: 55.6 us -> 1.35 us
  local copies, waits for them, and re-layouts: 2.1 us -> 39.2 us
  between operations: 13.5 us -> 0.14 us
  blocking collectives: 0 us -> 11.6 us
  other arithmetic: 7.2 us -> 1.21 us
  starting transfers between devices: 14.1 us -> 8.37 us
    reduce_scatter x1 -> x0, waiting for transfers between devices: 113 us -> none  [shards(): lax.psum_scatter(jnp.dot(picked, w_out, preferred_element_type=jnp.float3...]
    pallas_call x0 -> x2, Pallas kernels: none -> 81.2 us  [the longest x1 44 us: project(): pl.pallas_call(functools.partial(project_kernel, Z, R, C, Kc), out_shape=...]
    all_gather x1 -> x0, waiting for transfers between devices: 55.5 us -> none  [shards(): gathered = lax.all_gather(normed, 'gx', axis=0, tiled=True)]
    dot_general x5 -> x0, matrix products: 52.7 us -> none  [the longest x1 24.2 us: shards(): jnp.dot(picked, w_down, preferred_element_type=jnp.float32)]
    unnamed x8 -> x16, local copies, waits for them, and re-layouts: 0.82 us -> 36.3 us
    all_to_all x3 -> x2, waiting for transfers between devices: 1.61 us -> 13.5 us  [the longest x1 8.62 us: shards(): lax.all_to_all(to_index_order(query_cols), 'gx', split_axis=0, concat_axi...]
    all_to_all x0 -> x1, blocking collectives: none -> 11.6 us  [shards(): lax.all_to_all(attended.reshape(R, n, -1).transpose(1, 0, 2), 'gx', split...]
    all_to_all x3 -> x2, starting transfers between devices: 13.8 us -> 8.37 us  [the longest x1 4.85 us: shards(): lax.all_to_all(to_index_order(keyval_cols), 'gx', split_axis=0, concat_ax...]
  transfers between devices with their start and end apart: 5 -> 2, of which waited for: 3 -> 2; matrix products, arithmetic and copies ran while one was open for 15% -> 1% of each run, Pallas kernels for 0% -> 0%
where the time goes in v1:
time: 158 us; the launch traced here: 157 us
  Pallas kernels  81.2 us (51%)
  local copies, waits for them, and re-layouts  39.2 us (25%)
  waiting for transfers between devices  13.5 us (9%)
  blocking collectives  11.6 us (7%)
  starting transfers between devices  8.37 us (5%)
    pallas_call x1, Pallas kernels, project(): pl.pallas_call(functools.partial(project_kernel, Z, R, C, Kc), out_shape=...  44 us
    pallas_call x1, Pallas kernels, combine(): pl.pallas_call(functools.partial(combine_kernel, Z, R, C, Kc), out_shape=...  37.2 us
    unnamed x16, local copies, waits for them, and re-layouts  36.3 us
    all_to_all x1, blocking collectives, shards(): lax.all_to_all(attended.reshape(R, n, -1).transpose(1, 0, 2), 'gx', split...  11.6 us
    all_to_all x1, waiting for transfers between devices, shards(): lax.all_to_all(to_index_order(query_cols), 'gx', split_axis=0, concat_axi...  8.62 us
    all_to_all x1, waiting for transfers between devices, shards(): lax.all_to_all(to_index_order(keyval_cols), 'gx', split_axis=0, concat_ax...  4.87 us
    all_to_all x1, starting transfers between devices, shards(): lax.all_to_all(to_index_order(keyval_cols), 'gx', split_axis=0, concat_ax...  4.85 us
    all_to_all x1, starting transfers between devices, shards(): lax.all_to_all(to_index_order(query_cols), 'gx', split_axis=0, concat_axi...  3.52 us
  transfers between devices with their start and end apart: 2, of which 2 were waited for; matrix products, arithmetic and copies ran while one was open for 1% of the time, Pallas kernels for 0%

profile of v1, /device:TPU:0, one launch (start us, length us, event | category | flops | bytes accessed | tf_op | source)
XLA Modules:
  0.0 156.6 jit_solution(6213931715296096141)
XLA Ops:
  0.0 0.0 copy-start
  0.0 15.8 %copy.24.wg = bf16[9216,576]{1,0:T(8,128)(2,1)} copy(bf16[9216,576]{0,1:T(8,128)(2,1)} %param.16) | data formatting | bytes 21233664 | tf_op args[5]
  15.8 15.7 %copy.25.wu = bf16[9216,576]{1,0:T(8,128)(2,1)} copy(bf16[9216,576]{0,1:T(8,128)(2,1)} %param.17) | data formatting | bytes 21233664 | tf_op args[6]
  31.5 0.0 copy-done.1
  31.5 1.9 %copy.23.wkv = bf16[9216,32]{1,0:T(8,128)(2,1)} copy(bf16[9216,32]{0,1:T(8,128)(2,1)S(1)} %copy-done.1) | data formatting | bytes 1179648 | tf_op args[3]
  33.4 44.0 %project.1 = (bf16[256,384]{1,0:T(8,128)(2,1)}, bf16[256,32]{1,0:T(8,128)(2,1)}, bf16[256,576]{1,0:T(8,128)(2,1)}) custom-call(bf16[16,9216]{1,0:T(8,128)(2,1)} %x_ref.3, f32[1,9216]{1,0:T(1,128)} %bitcast.34, bf16[9216,384]{1,0:T(8,128)(2,1)} %wq.1, bf16[9216,32]{1,0:T(8,128)(2,1)} %copy.23.wkv, bf16[9216,576]{1,0:T(8,128)(2,1)} %copy.24.wg, ...), custom_call_target="tpu_custom_call" | custom-call | tf_op jit(solution)/shard_map/project/pallas_call | solution.py:191
  77.3 0.8 copy.28
  78.2 0.7 reshape.63
  78.9 4.8 %all-to-all-start.1 = ((bf16[16,2,256]{2,1,0:T(2,128)(2,1)}), bf16[16,2,256]{2,1,0:T(2,128)(2,1)S(1)}, u32[]{:S(2)}, u32[]{:S(2)}) async-start(bf16[16,2,256]{2,1,0:T(2,128)(2,1)} %reshape.63), calls=%async_computation.1 | async-start | bytes 32768 | tf_op jit(solution)/shard_map/all_to_all | solution.py:430
  83.8 1.6 %copy.26 = bf16[2,2,4,16,384]{4,3,0,1,2:T(8,128)(2,1)} copy(bf16[2,2,4,16,384]{4,3,2,1,0:T(8,128)(2,1)} %bitcast.32) | data formatting | bytes 393216 | tf_op jit(solution)/shard_map/reshape | solution.py:425
  85.4 4.9 %all-to-all-done.1 = bf16[16,2,256]{2,1,0:T(2,128)(2,1)S(1)} async-done(((bf16[16,2,256]{2,1,0:T(2,128)(2,1)}), bf16[16,2,256]{2,1,0:T(2,128)(2,1)S(1)}, u32[]{:S(2)}, u32[]{:S(2)}) %all-to-all-start.1) | async-done | bytes 16416 | tf_op jit(solution)/shard_map/all_to_all | solution.py:430
  90.3 3.5 %all-to-all-start = ((bf16[16,16,384]{2,1,0:T(8,128)(2,1)}), bf16[16,16,384]{2,1,0:T(8,128)(2,1)S(1)}, u32[]{:S(2)}, u32[]{:S(2)}) async-start(bf16[16,16,384]{2,1,0:T(8,128)(2,1)} %bitcast.3), calls=%async_computation | async-start | bytes 393216 | tf_op jit(solution)/shard_map/all_to_all | solution.py:429
  93.8 0.0 copy-done.3
  93.8 0.1 iota_compare_fusion
  93.9 0.1 reshape.64
  94.0 0.1 reshape.58
  94.1 8.6 %all-to-all-done = bf16[16,16,384]{2,1,0:T(8,128)(2,1)S(1)} async-done(((bf16[16,16,384]{2,1,0:T(8,128)(2,1)}), bf16[16,16,384]{2,1,0:T(8,128)(2,1)S(1)}, u32[]{:S(2)}, u32[]{:S(2)}) %all-to-all-start) | async-done | bytes 196640 | tf_op jit(solution)/shard_map/all_to_all | solution.py:429
  102.8 0.1 reshape.55
  102.9 0.0 copy-start.4
  102.9 0.2 fusion.5
  103.1 0.0 copy-done
  103.1 0.7 fusion.9
  103.9 0.2 fusion.2
  104.1 0.0 copy-start.2
  104.1 0.4 copy-done.4
  104.5 0.4 fusion.1
  105.0 0.1 convert_element_type.24
  105.1 11.6 %all_to_all.15 = bf16[16,16,384]{2,1,0:T(8,128)(2,1)S(1)} all-to-all(bf16[16,16,384]{2,1,0:T(8,128)(2,1)S(1)} %bitcast.28), channel_id=1, replica_groups=mesh['grp'=2,'gx'=16] {'gx'}, dimensions={0} | all-to-all | bytes 393216 | tf_op jit(solution)/shard_map/all_to_all | solution.py:438
  116.8 0.0 copy-done.2
  116.8 0.9 pad_maximum_fusion.lhs_ref
  117.6 37.2 %combine.1 = bf16[16,9216]{1,0:T(8,128)(2,1)} custom-call(bf16[16,9216]{1,0:T(8,128)(2,1)} %x_ref.3, bf16[256,960]{1,0:T(8,128)(2,1)} %pad_maximum_fusion.lhs_ref, bf16[384,9216]{1,0:T(8,128)(2,1)} %wo.1, bf16[576,9216]{1,0:T(8,128)(2,1)} %wd.1), custom_call_target="tpu_custom_call" | custom-call | tf_op jit(solution)/shard_map/combine/pallas_call | solution.py:349
  154.9 1.7 %copy.39 = bf16[16,9216]{1,0:T(8,128)(2,1)} copy(bf16[16,9216]{1,0:T(8,128)(2,1)} %combine.1) | data formatting | bytes 589824
  (9 shorter events, 0.1 us)
Async XLA Ops:
  0.0 103.1 %copy-start = (bf16[16,256,256]{2,1,0:T(8,128)(2,1)S(1)}, bf16[16,256,256]{2,1,0:T(8,128)(2,1)}, u32[]{:S(2)}) copy-start(bf16[16,256,256]{2,1,0:T(8,128)(2,1)} %param.19) | copy-start | bytes 6291460
  15.8 15.7 %copy-start.1 = (bf16[9216,32]{0,1:T(8,128)(2,1)S(1)}, bf16[9216,32]{0,1:T(8,128)(2,1)}, u32[]{:S(2)}) copy-start(bf16[9216,32]{0,1:T(8,128)(2,1)} %param.14) | copy-start | bytes 1769476
  33.4 60.4 %copy-start.3 = (s32[16]{0:T(128)S(1)}, s32[16]{0:T(128)}, u32[]{:S(2)}) copy-start(s32[16]{0:T(128)} %param.21) | copy-start | bytes 196
  78.9 11.4 %all-to-all-start.1 = ((bf16[16,2,256]{2,1,0:T(2,128)(2,1)}), bf16[16,2,256]{2,1,0:T(2,128)(2,1)S(1)}, u32[]{:S(2)}, u32[]{:S(2)}) async-start(bf16[16,2,256]{2,1,0:T(2,128)(2,1)} %reshape.63), calls=%async_computation.1 | async-start | bytes 32768 | tf_op jit(solution)/shard_map/all_to_all | solution.py:430
  90.3 12.5 %all-to-all-start = ((bf16[16,16,384]{2,1,0:T(8,128)(2,1)}), bf16[16,16,384]{2,1,0:T(8,128)(2,1)S(1)}, u32[]{:S(2)}, u32[]{:S(2)}) async-start(bf16[16,16,384]{2,1,0:T(8,128)(2,1)} %bitcast.3), calls=%async_computation | async-start | bytes 393216 | tf_op jit(solution)/shard_map/all_to_all | solution.py:429
  102.9 1.6 %copy-start.4 = (bf16[16,256,256]{2,1,0:T(8,128)(2,1)S(1)}, bf16[16,256,256]{2,1,0:T(8,128)(2,1)}, u32[]{:S(2)}) copy-start(bf16[16,256,256]{2,1,0:T(8,128)(2,1)} %param.20) | copy-start | bytes 6291460
  104.1 12.7 %copy-start.2 = (bf16[256,576]{1,0:T(8,128)(2,1)S(1)}, bf16[256,576]{1,0:T(8,128)(2,1)}, u32[]{:S(2)}) copy-start(bf16[256,576]{1,0:T(8,128)(2,1)} %get-tuple-element.10) | copy-start | bytes 884740

commit v2 on v1

--- a/solution.py
+++ b/solution.py
@@ -29,9 +29,14 @@
     return out + [index_of(z, 1 - y, c), index_of(z, y, 1 - c)]
 
 
-def greet(Z, z, y, c):
+def greet(Z, z, y, c, everyone=False):
     barrier = pltpu.get_barrier_semaphore()
-    for p in partners(Z, z, y, c):
+    me = index_of(z, y, c)
+    if everyone:
+        all_partners = [lax.rem(me + d, 4 * Z) for d in range(1, 4 * Z)]
+    else:
+        all_partners = partners(Z, z, y, c)
+    for p in all_partners:
         pl.semaphore_signal(
             barrier, inc=1, device_id={"gx": p}, device_id_type=pl.DeviceIdType.MESH
         )
@@ -52,7 +57,7 @@
 def project_kernel(
     Z, R, C, Kc,
     x_ref, gain_ref, wq, wkv, wg, wu,
-    q_out, kv_out, hid_out,
+    qkv_out, hid_out,
     gbuf, wqb, wkvb, wgb, wub, accq, acckv, accg, accu,
     zsend, zrecv, ysend, yrecv, csend, crecv, wsem,
 ):
@@ -64,9 +69,9 @@
 
     def wcopy(k, i):
         src, dst = weights[i]
-        return pltpu.make_async_copy(
-            src.at[pl.ds(pl.multiple_of(k * Kc, Kc), Kc), :], dst.at[k], wsem.at[k, i]
-        )
+        part = pl.ds(pl.multiple_of(k * Kc, Kc), Kc)
+        src = src.at[part, :] if i == 0 else src.at[:, part]
+        return pltpu.make_async_copy(src, dst.at[k], wsem.at[k, i])
 
     def wstart(k):
         for i in range(4):
@@ -156,15 +161,20 @@
             for i in range(4):
                 wcopy(k, i).wait()
             rows = gbuf[k]
-            for acc, w in ((accq, wqb), (acckv, wkvb), (accg, wgb), (accu, wub)):
-                acc[...] += jnp.dot(rows, w[k], preferred_element_type=jnp.float32)
+            accq[...] += jnp.dot(rows, wqb[k], preferred_element_type=jnp.float32)
+            for acc, w in ((acckv, wkvb), (accg, wgb), (accu, wub)):
+                acc[...] += lax.dot_general(
+                    rows, w[k], (((1,), (1,)), ((), ())), preferred_element_type=jnp.float32
+                )
 
         return carry
 
     lax.fori_loop(0, C + LY + LC, step, 0)
 
-    q_out[...] = accq[...].astype(jnp.bfloat16)
-    kv_out[...] = acckv[...].astype(jnp.bfloat16)
+    nq, nkv, wide = accq.shape[1], acckv.shape[1], qkv_out.shape[1]
+    qkv_out[...] = jnp.zeros_like(qkv_out)
+    qkv_out[:, 0:nq] = accq[...].astype(jnp.bfloat16)
+    qkv_out[:, wide - 128 : wide - 128 + nkv] = acckv[...].astype(jnp.bfloat16)
     gate = accg[...]
     hid_out[...] = (gate * jax.nn.sigmoid(gate) * accu[...]).astype(jnp.bfloat16)
 
@@ -191,18 +201,17 @@
     return pl.pallas_call(
         functools.partial(project_kernel, Z, R, C, Kc),
         out_shape=[
-            jax.ShapeDtypeStruct((N, nq), bf),
-            jax.ShapeDtypeStruct((N, nkv), bf),
+            jax.ShapeDtypeStruct((N, -(-nq // 128) * 128 + 128), bf),
             jax.ShapeDtypeStruct((N, ng), bf),
         ],
         in_specs=[vmem, vmem, hbm, hbm, hbm, hbm],
-        out_specs=[vmem, vmem, vmem],
+        out_specs=[vmem, vmem],
         scratch_shapes=[
             pltpu.VMEM((C, N, Kc), bf),
             pltpu.VMEM((C, Kc, nq), bf),
-            pltpu.VMEM((C, Kc, nkv), bf),
-            pltpu.VMEM((C, Kc, ng), bf),
-            pltpu.VMEM((C, Kc, ng), bf),
+            pltpu.VMEM((C, nkv, Kc), bf),
+            pltpu.VMEM((C, ng, Kc), bf),
+            pltpu.VMEM((C, ng, Kc), bf),
             pltpu.VMEM((N, nq), f32),
             pltpu.VMEM((N, nkv), f32),
             pltpu.VMEM((N, ng), f32),
@@ -219,18 +228,157 @@
             collective_id=0, has_side_effects=True, vmem_limit_bytes=56 * MIB
         ),
         name="project",
-    )(x, gain.reshape(1, D), wq, wkv, wg, wu)
+    )(x, gain.reshape(1, D), wq, wkv.T, wg.T, wu.T)
+
+
+def attend(
+    Z, R, z, y, c,
+    qkv_ref, keys, values, len_ref, lhs_ref,
+    qrecv, qall, score, prob, att, asend, keyb, valb,
+    q_send, q_recv, a_send, a_recv, kv_sem,
+    barrier,
+):
+    n = 4 * Z
+    me = index_of(z, y, c)
+    L = keyb.shape[1]
+    nq = asend.shape[2]
+    nkv = 2 * HD // n
+    per = nq // 128
+    M = H * R
+    bf, f32 = jnp.bfloat16, jnp.float32
+    kcopy = pltpu.make_async_copy(keys, keyb, kv_sem.at[0])
+    vcopy = pltpu.make_async_copy(values, valb, kv_sem.at[1])
+    kcopy.start()
+    vcopy.start()
+
+    def row_of(p):
+        place = (lax.rem(p, 2) * 2 + lax.rem(lax.div(p, 2), 2)) * Z + lax.div(p, 4)
+        return pl.multiple_of(place * R, R)
+
+    def qcopy(d):
+        to = lax.rem(me + d, n)
+        return remote(
+            qkv_ref.at[pl.ds(row_of(to), R), :], qrecv.at[me], q_send.at[d], q_recv.at[d], to
+        )
+
+    def qarrival(d):
+        source = lax.rem(me + n - d, n)
+        return remote(
+            qkv_ref.at[pl.ds(row_of(me), R), :],
+            qrecv.at[source],
+            q_send.at[d],
+            q_recv.at[d],
+            lax.rem(me + d, n),
+        )
+
+    def acopy(d):
+        to = lax.rem(me + d, n)
+        return remote(
+            asend.at[to],
+            lhs_ref.at[pl.ds(row_of(me), R), pl.ds(0, nq)],
+            a_send.at[d],
+            a_recv.at[d],
+            to,
+        )
+
+    def aarrival(d):
+        source = lax.rem(me + n - d, n)
+        return remote(
+            asend.at[me],
+            lhs_ref.at[pl.ds(row_of(source), R), pl.ds(0, nq)],
+            a_send.at[d],
+            a_recv.at[d],
+            lax.rem(me + d, n),
+        )
+
+    def each(f):
+        def body(d, carry):
+            f(d)
+            return carry
+
+        lax.fori_loop(1, n, body, 0)
+
+    pl.semaphore_wait(barrier, n - 1)
+    each(lambda d: qcopy(d).start())
+    qrecv[me] = qkv_ref[pl.ds(row_of(me), R), :]
+    each(lambda d: qarrival(d).wait_recv())
+
+    for b in range(2 * H):
+        qall[(b // 2) * R : (b // 2 + 1) * R, (b % 2) * 128 : (b % 2 + 1) * 128] = qrecv[
+            b // per, :, (b % per) * 128 : (b % per + 1) * 128
+        ]
+    wide = qrecv.shape[2]
+    pieces = [qrecv[p, :, wide - 128 :].astype(f32)[:, :nkv] for p in range(n)]
+    new_key = jnp.concatenate(pieces[: n // 2], axis=1)
+    new_value = jnp.concatenate(pieces[n // 2 :], axis=1)
+
+    row_in_head = lax.rem(lax.broadcasted_iota(jnp.int32, (M, L), 0), R)
+    kcopy.wait()
+
+    def score_row(r, carry):
+        s = lax.dot_general(
+            qall[...], keyb[r], (((1,), (1,)), ((), ())), preferred_element_type=f32
+        )
+        score[...] = jnp.where(row_in_head == r, s, score[...])
+        return carry
+
+    score[...] = jnp.zeros_like(score)
+    lax.fori_loop(0, R, score_row, 0)
+
+    live = lax.broadcasted_iota(jnp.int32, (R, L), 1) < len_ref[...]
+    for h in range(H):
+        rows = slice(h * R, (h + 1) * R)
+        s = jnp.where(live, score[rows, :] / 16.0, -1e30)
+        own = jnp.sum(qall[rows, :].astype(f32) * new_key, axis=1, keepdims=True) / 16.0
+        highest = jnp.maximum(jnp.max(s, axis=1, keepdims=True), own)
+        weights = jnp.exp(s - highest)
+        own_weight = jnp.exp(own - highest)
+        denominator = jnp.sum(weights, axis=1, keepdims=True) + own_weight
+        prob[rows, :] = (weights / denominator).astype(bf).astype(f32)
+        own_prob = (own_weight / denominator).astype(bf).astype(f32)
+        att[rows, :] = own_prob * new_value
+
+    vcopy.wait()
+
+    def value_row(r, carry):
+        p = jnp.where(row_in_head == r, prob[...], 0.0).astype(bf)
+        att[...] += jnp.dot(p, valb[r], preferred_element_type=f32)
+        return carry
+
+    lax.fori_loop(0, R, value_row, 0)
+
+    for b in range(2 * H):
+        asend[b // per, :, (b % per) * 128 : (b % per + 1) * 128] = att[
+            (b // 2) * R : (b // 2 + 1) * R, (b % 2) * 128 : (b % 2 + 1) * 128
+        ].astype(bf)
+    each(lambda d: acopy(d).start())
+    lhs_ref[pl.ds(row_of(me), R), pl.ds(0, nq)] = asend[me]
+    each(lambda d: aarrival(d).wait_recv())
+
+    def drain():
+        each(lambda d: qcopy(d).wait_send())
+        each(lambda d: acopy(d).wait_send())
+
+    return drain
 
 
 def combine_kernel(
-    Z, R, C, Kc,
-    x_ref, lhs_ref, wo, wd,
-    out_ref,
-    wbuf, part, lineb, ownb, csb, crb, ysb, yrb, zsb, zrb,
-    zsend, zrecv, ysend, yrecv, csend, crecv, wsem,
+    Z, R, C, Kc, fused,
+    x_ref, *refs,
 ):
+    if fused:
+        qkv_ref, hid_ref, keys, values, len_ref, wo, wd, out_ref, lhs_ref = refs[:9]
+        attend_scratch = refs[9:22]
+        refs = refs[22:]
+    else:
+        lhs_ref, wo, wd, out_ref = refs[:4]
+        refs = refs[4:]
+    (
+        wbuf, part, lineb, ownb, csb, crb, ysb, yrb, zsb, zrb,
+        zsend, zrecv, ysend, yrecv, csend, crecv, wsem,
+    ) = refs
     z, y, c = places(Z)
-    barrier = greet(Z, z, y, c)
+    barrier = greet(Z, z, y, c, fused)
     no, nd = wo.shape[0], wd.shape[0]
     AHEAD = 4
     LC, LY, LZ = 1, 2, 2
@@ -271,7 +419,13 @@
             index_of(to, y, c),
         )
 
-    pl.semaphore_wait(barrier, Z + 1)
+    if fused:
+        lhs_ref[:, no:] = hid_ref[...]
+        finish = attend(
+            Z, R, z, y, c, qkv_ref, keys, values, len_ref, lhs_ref, *attend_scratch, barrier
+        )
+    else:
+        pl.semaphore_wait(barrier, Z + 1)
 
     def step(s, carry):
         @pl.when(s + AHEAD < C)
@@ -335,9 +489,12 @@
         return carry
 
     lax.fori_loop(0, C, drain, 0)
-
-
-def combine(n, x, lhs, wo, wd):
+    if fused:
+        finish()
+
+
+def combine(n, x, operands, wo, wd):
+    fused = len(operands) > 1
     R, D = x.shape
     Z = n // 4
     Kc = 1024
@@ -346,13 +503,35 @@
     vmem = pl.BlockSpec(memory_space=pltpu.VMEM)
     hbm = pl.BlockSpec(memory_space=pl.ANY)
     bf, f32 = jnp.bfloat16, jnp.float32
+    nq, nin = wo.shape[0], wo.shape[0] + wd.shape[0]
+    extra = []
+    if fused:
+        qkv, _, keys, _, _ = operands
+        L = keys.shape[1]
+        extra = [
+            pltpu.VMEM((N, nin), bf),
+            pltpu.VMEM((n, R, qkv.shape[1]), bf),
+            pltpu.VMEM((H * R, HD), bf),
+            pltpu.VMEM((H * R, L), f32),
+            pltpu.VMEM((H * R, L), f32),
+            pltpu.VMEM((H * R, HD), f32),
+            pltpu.VMEM((n, R, nq), bf),
+            pltpu.VMEM((R, L, HD), bf),
+            pltpu.VMEM((R, L, HD), bf),
+            pltpu.SemaphoreType.DMA((n,)),
+            pltpu.SemaphoreType.DMA((n,)),
+            pltpu.SemaphoreType.DMA((n,)),
+            pltpu.SemaphoreType.DMA((n,)),
+            pltpu.SemaphoreType.DMA((2,)),
+        ]
     return pl.pallas_call(
-        functools.partial(combine_kernel, Z, R, C, Kc),
+        functools.partial(combine_kernel, Z, R, C, Kc, fused),
         out_shape=jax.ShapeDtypeStruct((R, D), bf),
-        in_specs=[vmem, vmem, hbm, hbm],
+        in_specs=[vmem] + ([vmem, vmem, hbm, hbm, vmem] if fused else [vmem]) + [hbm, hbm],
         out_specs=vmem,
-        scratch_shapes=[
-            pltpu.VMEM((C, lhs.shape[1], Kc), bf),
+        scratch_shapes=extra
+        + [
+            pltpu.VMEM((C, nin, Kc), bf),
             pltpu.VMEM((4, N, Kc), f32),
             pltpu.VMEM((4, Z * R, Kc), f32),
             pltpu.VMEM((4, R, Kc), f32),
@@ -374,7 +553,7 @@
             collective_id=1, has_side_effects=True, vmem_limit_bytes=56 * MIB
         ),
         name="combine",
-    )(x, lhs, wo, wd)
+    )(x, *operands, wo, wd)
 
 
 def block_scores(queries, key_block, lengths):
@@ -417,9 +596,13 @@
 ):
     R = layer_input.shape[0]
     Z = n // 4
-    query_cols, keyval_cols, hidden = project(
-        n, layer_input, norm_gain, w_query, w_keyval, w_gate, w_up
-    )
+    qkv, hidden = project(n, layer_input, norm_gain, w_query, w_keyval, w_gate, w_up)
+    nq, nkv = w_query.shape[1], w_keyval.shape[1]
+    if nq % 128 == 0 and w_out.shape[0] == nq:
+        operands = (qkv, hidden, cache_keys, cache_values, lengths.reshape(R, 1))
+        return combine(n, layer_input, operands, w_out, w_down)
+    query_cols = qkv[:, :nq]
+    keyval_cols = qkv[:, qkv.shape[1] - 128 :][:, :nkv]
 
     def to_index_order(a):
         a = a.reshape(2, 2, Z, R, a.shape[1]).transpose(2, 1, 0, 3, 4)
@@ -440,7 +623,7 @@
     )
     att = att.reshape(Z, 2, 2, R, -1).transpose(2, 1, 0, 3, 4).reshape(n * R, -1)
     lhs = jnp.concatenate([att, hidden], axis=1)
-    return combine(n, layer_input, lhs, w_out, w_down)
+    return combine(n, layer_input, (lhs,), w_out, w_down)
 
 
 def solution(mesh):

time: 158 us -> 110 us (0.70)
  local copies, waits for them, and re-layouts: 39.2 us -> 3.02 us
  Pallas kernels: 81.2 us -> 106 us
  waiting for transfers between devices: 13.5 us -> 0 us
  blocking collectives: 11.6 us -> 0 us
  starting transfers between devices: 8.37 us -> 0 us
    unnamed x16 -> x1, local copies, waits for them, and re-layouts: 36.3 us -> 1.69 us
    pallas_call x1, Pallas kernels: 37.2 us -> 62.4 us  [combine(): pl.pallas_call(functools.partial(combine_kernel, Z, R, C, Kc, fused), out...]
    all_to_all x2 -> x0, waiting for transfers between devices: 13.5 us -> none  [the longest x1 8.62 us: shards(): lax.all_to_all(to_index_order(query_cols), 'gx', split_axis=0, concat_axi...]
    all_to_all x1 -> x0, blocking collectives: 11.6 us -> none  [shards(): lax.all_to_all(attended.reshape(R, n, -1).transpose(1, 0, 2), 'gx', split...]
    all_to_all x2 -> x0, starting transfers between devices: 8.37 us -> none  [the longest x1 4.85 us: shards(): lax.all_to_all(to_index_order(keyval_cols), 'gx', split_axis=0, concat_ax...]
  transfers between devices with their start and end apart: 2 -> 0, of which waited for: 2 -> 0; matrix products, arithmetic and copies ran while one was open for 1% -> 0% of each run, Pallas kernels for 0% -> 0%
where the time goes in v2:
time: 110 us; the launch traced here: 109 us
  Pallas kernels  106 us (96%)
  local copies, waits for them, and re-layouts  3.02 us (3%)
    pallas_call x1, Pallas kernels, combine(): pl.pallas_call(functools.partial(combine_kernel, Z, R, C, Kc, fused), out...  62.4 us
    pallas_call x1, Pallas kernels, project(): pl.pallas_call(functools.partial(project_kernel, Z, R, C, Kc), out_shape=...  43.9 us

profile of v2, /device:TPU:0, one launch (start us, length us, event | category | flops | bytes accessed | tf_op | source)
XLA Modules:
  0.0 109.4 jit_solution(8945331476098877023)
XLA Ops:
  0.0 1.3 %copy.12.refs_4_ = s32[16,1]{1,0:T(8,128)} copy(s32[16,1]{0,1:T(1,128)} %bitcast.9) | data formatting | bytes 128 | tf_op jit(solution)/shard_map/reshape | solution.py:602
  1.3 43.9 %project.1 = (bf16[256,512]{1,0:T(8,128)(2,1)}, bf16[256,576]{1,0:T(8,128)(2,1)}) custom-call(bf16[16,9216]{1,0:T(8,128)(2,1)} %x_ref.3, f32[1,9216]{1,0:T(1,128)} %bitcast.8, bf16[9216,384]{1,0:T(8,128)(2,1)} %wq.1, bf16[32,9216]{1,0:T(8,128)(2,1)} %bitcast.7, bf16[576,9216]{1,0:T(8,128)(2,1)} %bitcast.5, bf16[576,9216]{1,0:T(8,128)(2,1)} %bitcast.6), custom_call_target="tpu_custom_call" | custom-call | tf_op jit(solution)/shard_map/project/pallas_call | solution.py:201
  45.3 62.4 %combine.1 = bf16[16,9216]{1,0:T(8,128)(2,1)} custom-call(bf16[16,9216]{1,0:T(8,128)(2,1)} %x_ref.3, bf16[256,512]{1,0:T(8,128)(2,1)} %get-tuple-element.7.refs_0_, bf16[256,576]{1,0:T(8,128)(2,1)} %get-tuple-element.8.refs_1_, bf16[16,256,256]{2,1,0:T(8,128)(2,1)} %refs_2_.1, bf16[16,256,256]{2,1,0:T(8,128)(2,1)} %refs_3_.1, s32[16,1]{1,0:T(8,128)} %copy.12.refs_4_, ...), custom_call_target="tpu_custom_call" | custom-call | tf_op jit(solution)/shard_map/combine/pallas_call | solution.py:527
  107.7 1.7 %copy.14 = bf16[16,9216]{1,0:T(8,128)(2,1)} copy(bf16[16,9216]{1,0:T(8,128)(2,1)} %combine.1) | data formatting | bytes 589824

commit v3 on v2

--- a/solution.py
+++ b/solution.py
@@ -292,11 +292,8 @@
         )
 
     def each(f):
-        def body(d, carry):
+        for d in sorted(range(1, n), key=lambda d: abs(n - 2 * d)):
             f(d)
-            return carry
-
-        lax.fori_loop(1, n, body, 0)
 
     pl.semaphore_wait(barrier, n - 1)
     each(lambda d: qcopy(d).start())
@@ -315,17 +312,25 @@
     row_in_head = lax.rem(lax.broadcasted_iota(jnp.int32, (M, L), 0), R)
     kcopy.wait()
 
-    def score_row(r, carry):
-        s = lax.dot_general(
-            qall[...], keyb[r], (((1,), (1,)), ((), ())), preferred_element_type=f32
-        )
-        score[...] = jnp.where(row_in_head == r, s, score[...])
+    def score_rows(i, carry):
+        picked = score[...]
+        for j in range(4):
+            r = i * 4 + j
+            s = lax.dot_general(
+                qall[...], keyb[r], (((1,), (1,)), ((), ())), preferred_element_type=f32
+            )
+            picked = jnp.where(row_in_head == r, s, picked)
+        score[...] = picked
         return carry
 
     score[...] = jnp.zeros_like(score)
-    lax.fori_loop(0, R, score_row, 0)
-
-    live = lax.broadcasted_iota(jnp.int32, (R, L), 1) < len_ref[...]
+    lax.fori_loop(0, R // 4, score_rows, 0)
+
+    row = lax.broadcasted_iota(jnp.int32, (R, L), 0)
+    length = jnp.zeros((R, L), jnp.int32)
+    for r in range(R):
+        length = jnp.where(row == r, len_ref[r], length)
+    live = lax.broadcasted_iota(jnp.int32, (R, L), 1) < length
     for h in range(H):
         rows = slice(h * R, (h + 1) * R)
         s = jnp.where(live, score[rows, :] / 16.0, -1e30)
@@ -340,12 +345,16 @@
 
     vcopy.wait()
 
-    def value_row(r, carry):
-        p = jnp.where(row_in_head == r, prob[...], 0.0).astype(bf)
-        att[...] += jnp.dot(p, valb[r], preferred_element_type=f32)
+    def value_rows(i, carry):
+        total = att[...]
+        for j in range(4):
+            r = i * 4 + j
+            p = jnp.where(row_in_head == r, prob[...], 0.0).astype(bf)
+            total = total + jnp.dot(p, valb[r], preferred_element_type=f32)
+        att[...] = total
         return carry
 
-    lax.fori_loop(0, R, value_row, 0)
+    lax.fori_loop(0, R // 4, value_rows, 0)
 
     for b in range(2 * H):
         asend[b // per, :, (b % per) * 128 : (b % per + 1) * 128] = att[
@@ -502,6 +511,7 @@
     N = n * R
     vmem = pl.BlockSpec(memory_space=pltpu.VMEM)
     hbm = pl.BlockSpec(memory_space=pl.ANY)
+    smem = pl.BlockSpec(memory_space=pltpu.SMEM)
     bf, f32 = jnp.bfloat16, jnp.float32
     nq, nin = wo.shape[0], wo.shape[0] + wd.shape[0]
     extra = []
@@ -527,7 +537,7 @@
     return pl.pallas_call(
         functools.partial(combine_kernel, Z, R, C, Kc, fused),
         out_shape=jax.ShapeDtypeStruct((R, D), bf),
-        in_specs=[vmem] + ([vmem, vmem, hbm, hbm, vmem] if fused else [vmem]) + [hbm, hbm],
+        in_specs=[vmem] + ([vmem, vmem, hbm, hbm, smem] if fused else [vmem]) + [hbm, hbm],
         out_specs=vmem,
         scratch_shapes=extra
         + [
@@ -599,7 +609,7 @@
     qkv, hidden = project(n, layer_input, norm_gain, w_query, w_keyval, w_gate, w_up)
     nq, nkv = w_query.shape[1], w_keyval.shape[1]
     if nq % 128 == 0 and w_out.shape[0] == nq:
-        operands = (qkv, hidden, cache_keys, cache_values, lengths.reshape(R, 1))
+        operands = (qkv, hidden, cache_keys, cache_values, lengths)
         return combine(n, layer_input, operands, w_out, w_down)
     query_cols = qkv[:, :nq]
     keyval_cols = qkv[:, qkv.shape[1] - 128 :][:, :nkv]

time: 110 us -> 104 us (0.945)
  Pallas kernels: 106 us -> 102 us
  local copies, waits for them, and re-layouts: 3.02 us -> 1.69 us
    pallas_call x1, Pallas kernels: 62.4 us -> 58.1 us  [combine(): pl.pallas_call(functools.partial(combine_kernel, Z, R, C, Kc, fused), out...]
    reshape x1 -> x0, local copies, waits for them, and re-layouts: 1.33 us -> none  [shards(): operands = (qkv, hidden, cache_keys, cache_values, lengths.reshape(R, 1))]
where the time goes in v3:
time: 104 us
  Pallas kernels  102 us (98%)
  local copies, waits for them, and re-layouts  1.69 us (2%)
    pallas_call x1, Pallas kernels, combine(): pl.pallas_call(functools.partial(combine_kernel, Z, R, C, Kc, fused), out...  58.1 us
    pallas_call x1, Pallas kernels, project(): pl.pallas_call(functools.partial(project_kernel, Z, R, C, Kc), out_shape=...  43.9 us

profile of v3, /device:TPU:0, one launch (start us, length us, event | category | flops | bytes accessed | tf_op | source)
XLA Modules:
  0.0 103.7 jit_solution(16423734930313611117)
XLA Ops:
  0.0 43.9 %project.1 = (bf16[256,512]{1,0:T(8,128)(2,1)}, bf16[256,576]{1,0:T(8,128)(2,1)}) custom-call(bf16[16,9216]{1,0:T(8,128)(2,1)} %x_ref.3, f32[1,9216]{1,0:T(1,128)} %bitcast.7, bf16[9216,384]{1,0:T(8,128)(2,1)} %wq.1, bf16[32,9216]{1,0:T(8,128)(2,1)} %bitcast.6, bf16[576,9216]{1,0:T(8,128)(2,1)} %bitcast.4, bf16[576,9216]{1,0:T(8,128)(2,1)} %bitcast.5), custom_call_target="tpu_custom_call" | custom-call | tf_op jit(solution)/shard_map/project/pallas_call | solution.py:201
  43.9 58.1 %combine.1 = bf16[16,9216]{1,0:T(8,128)(2,1)} custom-call(bf16[16,9216]{1,0:T(8,128)(2,1)} %x_ref.3, bf16[256,512]{1,0:T(8,128)(2,1)} %get-tuple-element.7.refs_0_, bf16[256,576]{1,0:T(8,128)(2,1)} %get-tuple-element.8.refs_1_, bf16[16,256,256]{2,1,0:T(8,128)(2,1)} %refs_2_.1, bf16[16,256,256]{2,1,0:T(8,128)(2,1)} %refs_3_.1, s32[16]{0:T(128)} %refs_4_.1, ...), custom_call_target="tpu_custom_call" | custom-call | tf_op jit(solution)/shard_map/combine/pallas_call | solution.py:537
  102.0 1.7 %copy.13 = bf16[16,9216]{1,0:T(8,128)(2,1)} copy(bf16[16,9216]{1,0:T(8,128)(2,1)} %combine.1) | data formatting | bytes 589824

commit v4 on v3

--- a/solution.py
+++ b/solution.py
@@ -314,8 +314,8 @@
 
     def score_rows(i, carry):
         picked = score[...]
-        for j in range(4):
-            r = i * 4 + j
+        for j in range(8):
+            r = i * 8 + j
             s = lax.dot_general(
                 qall[...], keyb[r], (((1,), (1,)), ((), ())), preferred_element_type=f32
             )
@@ -324,7 +324,7 @@
         return carry
 
     score[...] = jnp.zeros_like(score)
-    lax.fori_loop(0, R // 4, score_rows, 0)
+    lax.fori_loop(0, R // 8, score_rows, 0)
 
     row = lax.broadcasted_iota(jnp.int32, (R, L), 0)
     length = jnp.zeros((R, L), jnp.int32)
@@ -347,14 +347,14 @@
 
     def value_rows(i, carry):
         total = att[...]
-        for j in range(4):
-            r = i * 4 + j
+        for j in range(8):
+            r = i * 8 + j
             p = jnp.where(row_in_head == r, prob[...], 0.0).astype(bf)
             total = total + jnp.dot(p, valb[r], preferred_element_type=f32)
         att[...] = total
         return carry
 
-    lax.fori_loop(0, R // 4, value_rows, 0)
+    lax.fori_loop(0, R // 8, value_rows, 0)
 
     for b in range(2 * H):
         asend[b // per, :, (b % per) * 128 : (b % per + 1) * 128] = att[

time: 104 us -> 103 us (level)
  no operation moved by 1% of the time
where the time goes in v4:
time: 103 us
  Pallas kernels  101 us (98%)
  local copies, waits for them, and re-layouts  1.69 us (2%)
    pallas_call x1, Pallas kernels, combine(): pl.pallas_call(functools.partial(combine_kernel, Z, R, C, Kc, fused), out...  57.3 us
    pallas_call x1, Pallas kernels, project(): pl.pallas_call(functools.partial(project_kernel, Z, R, C, Kc), out_shape=...  43.9 us

profile of v4, /device:TPU:0, one launch (start us, length us, event | category | flops | bytes accessed | tf_op | source)
XLA Modules:
  0.0 103.0 jit_solution(13223496776040544467)
XLA Ops:
  0.0 43.9 %project.1 = (bf16[256,512]{1,0:T(8,128)(2,1)}, bf16[256,576]{1,0:T(8,128)(2,1)}) custom-call(bf16[16,9216]{1,0:T(8,128)(2,1)} %x_ref.3, f32[1,9216]{1,0:T(1,128)} %bitcast.7, bf16[9216,384]{1,0:T(8,128)(2,1)} %wq.1, bf16[32,9216]{1,0:T(8,128)(2,1)} %bitcast.6, bf16[576,9216]{1,0:T(8,128)(2,1)} %bitcast.4, bf16[576,9216]{1,0:T(8,128)(2,1)} %bitcast.5), custom_call_target="tpu_custom_call" | custom-call | tf_op jit(solution)/shard_map/project/pallas_call | solution.py:201
  43.9 57.3 %combine.1 = bf16[16,9216]{1,0:T(8,128)(2,1)} custom-call(bf16[16,9216]{1,0:T(8,128)(2,1)} %x_ref.3, bf16[256,512]{1,0:T(8,128)(2,1)} %get-tuple-element.7.refs_0_, bf16[256,576]{1,0:T(8,128)(2,1)} %get-tuple-element.8.refs_1_, bf16[16,256,256]{2,1,0:T(8,128)(2,1)} %refs_2_.1, bf16[16,256,256]{2,1,0:T(8,128)(2,1)} %refs_3_.1, s32[16]{0:T(128)} %refs_4_.1, ...), custom_call_target="tpu_custom_call" | custom-call | tf_op jit(solution)/shard_map/combine/pallas_call | solution.py:537
  101.3 1.7 %copy.13 = bf16[16,9216]{1,0:T(8,128)(2,1)} copy(bf16[16,9216]{1,0:T(8,128)(2,1)} %combine.1) | data formatting | bytes 589824
